TPU v7x, 128 devices: a whole 4x4x4 slice. The times are simulated.
128 devices in a mesh: tm: 16 (over y, x_lo, core), space: 8 (over x_hi, z).
Axes of the slice: x: 4 (x_hi: 2, x_lo: 2; x = x_hi * 2 + x_lo), y: 4, z: 4, core: 2. Of those that a mesh axis runs over, the one named last changes fastest.
Arguments:
- snapshots: bfloat16 [16384, 65536], P('space', 'tm'), may hold values from -60 to 60
- basis: bfloat16 [16384, 64], P('space'), may hold values from -0.046875 to 0.046875
Outputs:
- reduced_rates: float32 [64, 65536], P(None, ('tm', 'space'))
- gram_quad: float32 [2080, 2080], P('tm', 'space')
- gram_side: float32 [65, 2145], replicated
- rhs: float32 [2145, 64], replicated
All inputs are finite; a program needn't handle non-finite values.
Results may differ from a plain program's by a relative error of at most 0.0003.
Values sent between devices are 32-bit elements; how exact they have to be, the bound alone decides.
A program may use at most 128 MiB of HBM per device.

v0:
```python
import jax
import jax.numpy as jnp
import numpy as np
from jax import lax
from jax.sharding import PartitionSpec as P


def padded_2(cells, sides, width):
    for axis, dim in sides:
        count = lax.axis_size(axis)
        ends = count - 1
        head = lax.slice_in_dim(cells, 0, width, axis=dim)
        tail = lax.slice_in_dim(cells, cells.shape[dim] - width, cells.shape[dim], axis=dim)
        cells = jnp.concatenate(
            [
                lax.ppermute(tail, axis, [(i, (i + 1) % count) for i in range(ends)]),
                cells,
                lax.ppermute(head, axis, [((i + 1) % count, i) for i in range(ends)]),
            ],
            axis=dim,
        )
    return cells


def rates_from(window, first, last):
    inner = window[:, 1:-1]
    left = jnp.where(first, 2.0 * inner[:, :1] - inner[:, 1:2], window[:, :1])
    right = jnp.where(last, 2.0 * inner[:, -1:] - inner[:, -2:-1], window[:, -1:])
    full = jnp.concatenate([left, inner, right], axis=1)
    return 0.5 * (full[:, 2:] - full[:, :-2])


def body(snapshots, basis):
    n_space = lax.axis_size("space")
    n_time = lax.axis_size("tm")
    space_idx = lax.axis_index("space")
    time_idx = lax.axis_index("tm")
    partial_proj = lax.dot_general(
        basis, snapshots, (((0,), (0,)), ((), ())), preferred_element_type=jnp.float32
    )
    slab = partial_proj.shape[1]
    width = slab // n_space
    summed = lax.psum(partial_proj, "space")
    padded = padded_2(summed, (("tm", 1),), 1)
    window = lax.dynamic_slice_in_dim(padded, space_idx * width, width + 2, 1)
    first = jnp.logical_and(time_idx == 0, space_idx == 0)
    last = jnp.logical_and(time_idx == n_time - 1, space_idx == n_space - 1)
    reduced = window[:, 1:-1]
    rates = rates_from(window, first, last)
    modes = reduced.shape[0]
    upper_i, upper_j = np.triu_indices(modes)
    quad = reduced[upper_i] * reduced[upper_j]
    side = jnp.concatenate([jnp.ones((1, width), jnp.float32), reduced], axis=0)
    feats = jnp.concatenate([quad, side], axis=0)
    scale = 1.0 / (slab * n_time)
    dims = (((1,), (1,)), ((), ()))
    high = lax.Precision.HIGHEST
    side_part = lax.dot_general(side, feats, dims, precision=high)
    rhs_part = lax.dot_general(feats, rates, dims, precision=high)
    side_total, rhs_total = lax.psum((side_part, rhs_part), ("tm", "space"))
    quad_part = lax.dot_general(quad, quad, dims, precision=high)
    row_block = lax.psum_scatter(quad_part, "tm", scatter_dimension=0, tiled=True)
    quad_block = lax.psum_scatter(row_block, "space", scatter_dimension=1, tiled=True)
    return (rates, quad_block * scale, side_total * scale, rhs_total * scale)


def solution(mesh):
    in_specs = (P("space", "tm"), P("space", None))
    out_specs = (P(None, ("tm", "space")), P("tm", "space"), P(), P())
    return jax.shard_map(body, mesh=mesh, in_specs=in_specs, out_specs=out_specs, check_vma=False)
```

profile of v0, /device:TPU:1, one launch (start us, length us, event | category | flops | bytes accessed | tf_op | source)
XLA Modules:
  0.0 654.6 jit_solution(12047642121125978018)
XLA Ops:
  7.3 0.9 copy-done
  8.1 9.8 %fusion.7 = f32[64,4096]{1,0:T(8,128)} fusion(bf16[2048,64]{0,1:T(8,128)(2,1)S(1)} %copy-done, bf16[2048,4096]{1,0:T(8,128)(2,1)} %param.6), kind=kOutput, calls=%fused_computation.23 | convolution fusion | flops 1073741824 | bytes 18087936 | tf_op jit(solution)/shard_map/dot_general | solution.py:38
  18.0 86.2 %all-reduce.9.cloned.1.call-done = f32[64,4096]{1,0:T(8,128)} async-done(((f32[64,4096]{1,0:T(8,128)}), f32[64,4096]{1,0:T(8,128)}) %all-reduce.9.cloned.1.call-update) | async-done | bytes 1048592 | tf_op jit(solution)/shard_map/psum | solution.py:43
  104.2 0.8 fusion.6
  105.0 7.7 %collective-permute-start = (f32[64,1]{1,0:T(8,128)S(1)}, f32[64,1]{1,0:T(8,128)S(1)}, u32[]{:S(2)}, u32[]{:S(2)}) collective-permute-start(f32[64,1]{1,0:T(8,128)S(1)} %get-tuple-element.9), channel_id=1, source_target_pairs={{0,8},{8,16},{16,24},{24,32},{32,40},{40,48},{48,56},{56,64},{64,7... | collective-permute-start | bytes 776 | tf_op jit(solution)/shard_map/ppermute | solution.py:16
  112.8 1.9 collective-permute-start.1
  114.7 3.3 collective-permute-done.1
  118.0 1.6 concatenate.17
  119.6 0.1 constant_dynamic-slice_fusion.1
  119.7 6.8 %gather_fusion = f32[2080,512]{1,0:T(8,128)} fusion(f32[64,512]{1,0:T(8,128)S(1)} %constant_dynamic-slice_fusion.1, s32[3072]{0:T(1024)S(1)} %pad_clamp_fusion.1), kind=kCustom, calls=%fused_computation | custom fusion | bytes 8528000 | tf_op jit(solution)/shard_map/gather | solution.py:52
  126.6 6.8 %gather_fusion.1 = f32[2080,512]{1,0:T(8,128)} fusion(f32[64,512]{1,0:T(8,128)S(1)} %constant_dynamic-slice_fusion.1, s32[3072]{0:T(1024)S(1)} %pad_clamp_fusion), kind=kCustom, calls=%fused_computation.1 | custom fusion | bytes 8528000 | tf_op jit(solution)/shard_map/gather | solution.py:52
  133.4 4.5 mul.41
  137.9 2.0 copy-done.2
  140.0 34.2 %fusion.8 = f32[2080,2080]{1,0:T(8,128)} fusion(f32[2080,512]{1,0:T(8,128)S(1)} %mul.41), kind=kOutput, calls=%fused_computation.24 | convolution fusion | flops 26581401600 | bytes 21565440 | tf_op jit(solution)/shard_map/dot_general | solution.py:61
  174.1 207.0 %fusion = f32[144,2080]{1,0:T(8,128)S(1)} fusion(f32[2080,2080]{1,0:T(8,128)} %fusion.8), kind=kCustom, calls=%all-reduce-scatter | all-reduce-scatter fusion | flops 4792321 | bytes 18504192
  381.1 4.4 collective-permute-start.2
  385.5 0.9 slice.57
  386.4 12.7 %concatenate.21 = f32[2145,512]{1,0:T(8,128)} concatenate(f32[2080,512]{1,0:T(8,128)} %copy-done.2, f32[1,512]{1,0:T(1,128)S(1)} %broadcast_in_dim.11, f32[64,512]{1,0:T(8,128)S(1)} %constant_dynamic-slice_fusion.1), dimensions={0} | concatenate | bytes 8785920 | tf_op jit(solution)/shard_map/concatenate | solution.py:54
  399.1 5.0 collective-permute-start.3
  404.1 0.1 dynamic-slice_select_fusion.1
  404.3 7.1 %fusion.1 = f32[65,2145]{1,0:T(8,128)} fusion(f32[2145,512]{1,0:T(8,128)} %concatenate.21, f32[64,512]{1,0:T(8,128)S(1)} %constant_dynamic-slice_fusion.1), kind=kOutput, calls=%fused_computation.5 | convolution fusion | flops 856627200 | bytes 5081732 | tf_op jit(solution)/shard_map/dot_general | solution.py:58
  411.3 0.1 fusion.4
  411.5 4.9 fusion.9
  416.4 0.6 dynamic-slice.13
  417.7 0.6 dynamic-slice.2
  419.0 12.0 %concatenate.22 = f32[354,2080]{1,0:T(8,128)} concatenate(f32[66,2080]{1,0:T(8,128)S(1)} %collective-permute-done.3, f32[144,2080]{1,0:T(8,128)} %collective-permute-done.2, f32[144,2080]{1,0:T(8,128)S(1)} %fusion), dimensions={0} | concatenate | bytes 5890560
  430.9 2.4 constant_dynamic-slice_fusion
  433.4 127.9 %all-reduce.13.cloned.1.call-done = (f32[65,2145]{1,0:T(8,128)}, f32[2145,64]{0,1:T(8,128)}) async-done(((f32[65,2145]{1,0:T(8,128)}, f32[2145,64]{0,1:T(8,128)}), (f32[65,2145]{1,0:T(8,128)}, f32[2145,64]{0,1:T(8,128)})) %all-reduce.13.cloned.1.call-update) | async-done | bytes 1106836 | tf_op jit(solution)/shard_map/psum | solution.py:60
  561.2 1.9 broadcast_multiply_fusion.1
  563.1 1.9 broadcast_multiply_fusion
  565.1 81.2 %all-reduce.11.cloned.1.call-done = f32[130,2080]{1,0:T(8,128)} async-done(((f32[130,2080]{1,0:T(8,128)}), f32[130,2080]{1,0:T(8,128)}) %all-reduce.11.cloned.1.call-update) | async-done | bytes 1081616
  646.3 1.8 dynamic-slice_multiply_fusion
  (28 shorter events, 0.2 us)
Async XLA Ops:
  7.2 1.0 copy-start
  7.2 10.8 %copy-start.6 = (s32[2080]{0:T(1024)S(1)}, s32[2080]{0:T(1024)}, u32[]{:S(2)}) copy-start(s32[2080]{0:T(1024)} %constant.44) | copy-start | bytes 24964
  7.2 10.8 %copy-start.5 = (s32[2080]{0:T(1024)S(1)}, s32[2080]{0:T(1024)}, u32[]{:S(2)}) copy-start(s32[2080]{0:T(1024)} %constant.45) | copy-start | bytes 24964
  7.2 97.0 %all-reduce.9.cloned.1.call-start = ((), (), s32[]{:S(2)}) async-start(), calls=%async_computation | async-start | bytes 2097152 | tf_op jit(solution)/shard_map/psum | solution.py:43
  17.9 543.3 %all-reduce.13.cloned.1.call-start = ((), (), s32[]{:S(2)}) async-start(), calls=%async_computation.2 | async-start | bytes 2367488 | tf_op jit(solution)/shard_map/psum | solution.py:60
  105.0 9.7 %collective-permute-start = (f32[64,1]{1,0:T(8,128)S(1)}, f32[64,1]{1,0:T(8,128)S(1)}, u32[]{:S(2)}, u32[]{:S(2)}) collective-permute-start(f32[64,1]{1,0:T(8,128)S(1)} %get-tuple-element.9), channel_id=1, source_target_pairs={{0,8},{8,16},{16,24},{24,32},{32,40},{40,48},{48,56},{56,64},{64,7... | collective-permute-start | bytes 776 | tf_op jit(solution)/shard_map/ppermute | solution.py:16
  112.8 5.2 collective-permute-start.1
  137.9 2.0 copy-start.2
  381.1 37.8 %collective-permute-start.2 = (f32[144,2080]{1,0:T(8,128)S(1)}, f32[144,2080]{1,0:T(8,128)}, u32[]{:S(2)}, u32[]{:S(2)}) collective-permute-start(f32[144,2080]{1,0:T(8,128)S(1)} %fusion), channel_id=1, source_target_pairs={{0,8},{8,16},{16,24},{24,32},{32,40},{40,48},{48,56},{56,64},{64,7... | collective-permute-start | bytes 3594248
  399.1 12.4 %copy-start.3 = (f32[2145,512]{1,0:T(8,128)S(1)}, f32[2145,512]{1,0:T(8,128)}, u32[]{:S(2)}) copy-start(f32[2145,512]{1,0:T(8,128)} %concatenate.21) | copy-start | bytes 13178884
  399.1 19.9 %collective-permute-start.3 = (f32[66,2080]{1,0:T(8,128)}, f32[66,2080]{1,0:T(8,128)S(1)}, u32[]{:S(2)}, u32[]{:S(2)}) collective-permute-start(f32[66,2080]{1,0:T(8,128)} %slice.57), channel_id=1, source_target_pairs={{0,16},{8,24},{16,32},{24,40},{32,48},{40,56},{48,64},{56,72},{64,... | collective-permute-start | bytes 1647368
  411.3 5.1 copy-start.7
  411.3 6.4 copy-start.8
  411.5 19.5 %copy-start.4 = (f32[64,512]{1,0:T(8,128)}, f32[64,512]{1,0:T(8,128)S(1)}, u32[]{:S(2)}) copy-start(f32[64,512]{1,0:T(8,128)S(1)} %fusion.4) | copy-start | bytes 393220
  416.4 229.9 %all-reduce.11.cloned.1.call-start = ((), (), s32[]{:S(2)}) async-start(), calls=%async_computation.1 | async-start | bytes 2367488
  418.9 229.1 %copy-start.1 = (bf16[2048,64]{0,1:T(8,128)(2,1)S(1)}, bf16[2048,64]{0,1:T(8,128)(2,1)}, u32[]{:S(2)}) copy-start(bf16[2048,64]{0,1:T(8,128)(2,1)} %param.7) | copy-start | bytes 786436
Sparse Core Ops, SparseCore 0:
  18.1 86.0 all-reduce.8
  416.5 144.7 all-reduce.12
  563.9 82.2 all-reduce.10
where the time goes:
time: 660 us; the launch traced here: 655 us
  waiting for transfers between devices  299 us (45%)
  blocking collectives  207 us (31%)
  matrix products  55.9 us (8%)
  local copies, waits for them, and re-layouts  48.2 us (7%)
  starting transfers between devices  19.2 us (3%)
  between operations  15.3 us (2%)
  other arithmetic  10.4 us (2%)
    unnamed x1, blocking collectives  207 us
    psum x1, waiting for transfers between devices, body(): side_total, rhs_total = lax.psum((side_part, rhs_part), ('tm', 'space'))  128 us
    psum x1, waiting for transfers between devices, body(): summed = lax.psum(partial_proj, 'space')  86.2 us
    unnamed x6, waiting for transfers between devices  81.2 us
    dot_general x1, matrix products, body(): quad_part = lax.dot_general(quad, quad, dims, precision=high)  34.2 us
    unnamed x23, local copies, waits for them, and re-layouts  19.4 us
    gather x2, local copies, waits for them, and re-layouts, body(): quad = reduced[upper_i] * reduced[upper_j]  13.6 us
  transfers between devices with their start and end apart: 7, of which 4 were waited for; matrix products, arithmetic and copies ran while one was open for 7% of the time, Pallas kernels for 0%

commit v1 on v0

v1 whole, which is shorter than its diff:
```python
import functools

import jax
import jax.numpy as jnp
import numpy as np
from jax import lax
from jax.experimental import pallas as pl
from jax.experimental.pallas import tpu as pltpu
from jax.sharding import PartitionSpec as P

F32 = jnp.float32
BF16 = jnp.bfloat16
MESH = pl.DeviceIdType.MESH
ROWS_BY_ROWS = (((1,), (1,)), ((), ()))

MODES = 64
SPACE = 8
TIMES = 16
BLOCK = 512
SLAB = SPACE * BLOCK
MINE = 272
SENT = 264


def pair_of(k):
    i = 0
    while k >= MODES - i:
        k -= MODES - i
        i += 1
    return i, i + k


def half_plan(row):
    block, inside = divmod(row, 128)
    runs = []
    for r in range(8):
        i, j = pair_of(130 * block + inside + r)
        if not runs or runs[-1][1] != i:
            at = j - r + 8
            runs.append((r, i, at % 8, at - at % 8))
    return runs


def build_plan():
    segments = []
    for row in range(0, 2048, 16):
        low, high = half_plan(row), half_plan(row + 8)
        pure = len(low) == 1 and len(high) == 1 and low[0][1:3] == high[0][1:3]
        if not pure:
            segments.append((row, 16, (low, high)))
            continue
        run = low[0]
        last = segments[-1] if segments else None
        if (
            last
            and not isinstance(last[2], tuple)
            and last[2][0] == list(run)[1]
            and last[2][1] == run[2]
            and last[2][2] + last[1] == run[3]
        ):
            segments[-1] = (last[0], last[1] + 16, last[2])
        else:
            segments.append((row, 16, [run[1], run[2], run[3]]))
    return segments


def kernel(
    snap, basis, rates_o, gram_o, lo_o,
    AH, AL, MH, ML, LH, LL, BT, XA, XS, LQ, sbuf, rbuf, accs, crecv, isend, irecv,
    accl, turn, lom, lor, los, LOA,
    snap_sem, rs_s, rs_r, ag_s, ag_r, halo_s, halo_r, core_s, core_r, ici_s, ici_r,
    lo_s, lo_r, lt_s, lt_r, lx_s, lx_r, lc_s, lc_r,
):
    a = lax.axis_index("tm")
    s = lax.axis_index("space")
    y, xl, c = a // 4, (a // 2) % 2, a % 2
    xh, z = s // 4, s % 4

    def space_to(o):
        return ((xh + o // 4) % 2) * 4 + (z + o % 4) % 4

    def space_from(o):
        return ((xh + 2 - o // 4) % 2) * 4 + (z + 4 - o % 4) % 4

    def chip_to(o):
        return ((y + o // 2) % 4) * 2 + (xl + o % 2) % 2

    def copy(src, dst, ss, rs, tm, sp):
        return pltpu.make_async_remote_copy(
            src_ref=src, dst_ref=dst, send_sem=ss, recv_sem=rs, device_id=(tm, sp), device_id_type=MESH
        )

    def loop(low, high, step):
        def inner(k, carry):
            step(k)
            return carry

        lax.fori_loop(low, high, inner, 0)

    barrier = pltpu.get_barrier_semaphore()
    loop(1, 8, lambda o: pl.semaphore_signal(barrier, inc=1, device_id=(a, space_to(o)), device_id_type=MESH))
    loop(1, 16, lambda o: pl.semaphore_signal(barrier, inc=1, device_id=((a + o) % 16, s), device_id_type=MESH))

    def fetch(k):
        cols = pl.ds(pl.multiple_of(BLOCK * space_to(7 - k), BLOCK), BLOCK)
        into = pl.ds(pl.multiple_of(BLOCK * k, BLOCK), BLOCK)
        return pltpu.make_async_copy(snap.at[:, cols], AH.at[:, into], snap_sem.at[k])

    loop(0, 8, lambda k: fetch(k).start())
    BT[...] = basis[...].astype(F32).T.astype(BF16)

    def project(k):
        fetch(k).wait()
        into = pl.ds(pl.multiple_of(BLOCK * k, BLOCK), BLOCK)
        sbuf[k] = jnp.dot(BT[...], AH[:, into], preferred_element_type=F32)

    def share(k):
        o = 7 - k
        return copy(sbuf.at[k], rbuf.at[o - 1], rs_s.at[o - 1], rs_r.at[o - 1], a, space_to(o))

    project(0)
    pl.semaphore_wait(barrier, 22)
    share(0).start()

    def middle(k):
        project(k)
        share(k).start()

    loop(1, 7, middle)
    project(7)

    def add_share(o):
        share(7 - o).wait_recv()
        sbuf[7] += rbuf[o - 1]

    loop(1, 8, add_share)
    XA[s + 1] = sbuf[7]

    def spread(o):
        mine = XA.at[s + 1]
        return copy(mine, mine, ag_s.at[o - 1], ag_r.at[o - 1], a, space_to(o))

    def arrival(o):
        theirs = XA.at[space_from(o) + 1]
        return copy(theirs, theirs, ag_s.at[o - 1], ag_r.at[o - 1], a, space_to(o))

    loop(1, 8, lambda o: spread(o).start())

    segments = build_plan()

    def split(value):
        high = value.astype(BF16)
        return high, (value - high.astype(F32)).astype(BF16)

    LQ[...] = jnp.where(lax.broadcasted_iota(jnp.int32, (64, BLOCK), 0) % 8 == 4, 1.0, 0.0).astype(F32)
    LH[192:256, :] = jnp.zeros((64, SLAB), BF16)
    LL[192:256, :] = jnp.zeros((64, SLAB), BF16)
    row8 = lax.broadcasted_iota(jnp.int32, (8, BLOCK), 0)

    def build(o):
        @pl.when(o > 0)
        def _():
            arrival(o).wait_recv()

        b = space_from(o)
        cols = pl.ds(pl.multiple_of(BLOCK * b, BLOCK), BLOCK)
        x = XA[b + 1]
        pad = jnp.zeros((8, BLOCK), F32)
        xp = jnp.concatenate([pad, x, pad], axis=0)
        XS[0] = xp
        for shift in range(1, 8):
            XS[shift] = pltpu.roll(xp, 80 - shift, 0)

        def row(i):
            return XA[b + 1, i : i + 1, :]

        def half(runs):
            value = None
            for first, i, shift, base in runs:
                term = row(i) * XS[shift, base : base + 8, :]
                value = term if value is None else jnp.where(row8 >= first, term, value)
            return value

        for first, count, what in segments:
            if isinstance(what, tuple):
                value = jnp.concatenate([half(what[0]), half(what[1])], axis=0)
            else:
                i, shift, base = what
                value = row(i) * XS[shift, base : base + count, :]
            high, low = split(value)
            AH[first : first + count, cols] = high
            AL[first : first + count, cols] = low
        for n in range(8):
            for q, k in enumerate((260 * n + 128, 260 * n + 129, 260 * n + 258, 260 * n + 259)):
                i, j = pair_of(k)
                LQ[8 * n + q : 8 * n + q + 1, :] = row(i) * row(j)
        high, low = split(x)
        LH[0:64, cols] = high
        LL[0:64, cols] = low
        high, low = split(LQ[...])
        LH[128:192, cols] = high
        LL[128:192, cols] = low
        at = pl.multiple_of(8 * s, 8)
        high, low = split(jnp.concatenate([LQ[pl.ds(at, 8), :], XA[b + 1, pl.ds(at, 8), :]], axis=0))
        MH[256:272, cols] = high
        ML[256:272, cols] = low

    loop(0, 8, build)

    up, down = (a + 1) % 16, (a + 15) % 16
    halo = (
        copy(XA.at[8, :, 384:512], XA.at[0, :, 384:512], halo_s.at[0], halo_r.at[0], up, s),
        copy(XA.at[1, :, 0:128], XA.at[9, :, 0:128], halo_s.at[1], halo_r.at[1], down, s),
    )
    halo[0].start()
    halo[1].start()
    own = pl.ds(pl.multiple_of(256 * s, 256), 256)
    MH[0:256, :] = AH[own, :]
    ML[0:256, :] = AL[own, :]
    halo[0].wait()
    halo[1].wait()
    tail = XA[0, :, 384:512]
    ghost = 2.0 * XA[1, :, 0:1] - XA[1, :, 1:2]
    XA[0, :, 384:512] = jnp.where(a == 0, jnp.broadcast_to(ghost, (64, 128)), tail)
    head = XA[9, :, 0:128]
    ghost = 2.0 * XA[8, :, 511:512] - XA[8, :, 510:511]
    XA[9, :, 0:128] = jnp.where(a == 15, jnp.broadcast_to(ghost, (64, 128)), head)
    lane = lax.broadcasted_iota(jnp.int32, (64, BLOCK), 1)

    def rates_of(b):
        x = XA[b + 1]
        before = jnp.where(lane == 0, jnp.broadcast_to(XA[b, :, 511:512], x.shape), pltpu.roll(x, 1, 1))
        after = jnp.where(lane == BLOCK - 1, jnp.broadcast_to(XA[b + 2, :, 0:1], x.shape), pltpu.roll(x, BLOCK - 1, 1))
        return 0.5 * (after - before)

    def rate_rows(b):
        cols = pl.ds(pl.multiple_of(BLOCK * b, BLOCK), BLOCK)
        high, low = split(rates_of(b))
        LH[64:128, cols] = high
        LL[64:128, cols] = low

    loop(0, 8, rate_rows)
    rates_o[...] = rates_of(s)

    def products(high, low):
        out = lax.dot_general(MH[...], high, ROWS_BY_ROWS, preferred_element_type=F32)
        out += lax.dot_general(ML[...], high, ROWS_BY_ROWS, preferred_element_type=F32)
        return out + lax.dot_general(MH[...], low, ROWS_BY_ROWS, preferred_element_type=F32)

    accl[...] = products(LH[...], LL[...])
    turn[0:272, :] = accl[:, 128:256]
    turn[272:384, :] = jnp.zeros((112, 128), F32)
    for k in range(3):
        turned = turn[128 * k : 128 * k + 128, :].T
        for t in range(16):
            lom[t, 32 + 8 * k : 40 + 8 * k, :] = turned[8 * (t // 2) : 8 * (t // 2) + 8, :]
    for t in range(16):
        lom[t, 0:16, :] = accl[16 * t : 16 * t + 16, 0:128]
        lom[t, 16:32, :] = accl[256:272, 0:128]

    def lo_share(o):
        to = (a + o) % 16
        return copy(lom.at[to], lor.at[o], lo_s.at[o - 1], lo_r.at[o - 1], to, s)

    def lo_times(o):
        part = LOA.at[0, a]
        return copy(part, part, lt_s.at[o - 1], lt_r.at[o - 1], (a + o) % 16, s)

    def lo_times_arrival(o):
        part = LOA.at[0, (a + 16 - o) % 16]
        return copy(part, part, lt_s.at[o - 1], lt_r.at[o - 1], (a + o) % 16, s)

    def lo_space(o):
        part = pl.ds(9 * c, 9)
        return copy(LOA.at[0, part], LOA.at[o, part], lx_s.at[o - 1], lx_r.at[o - 1], a, space_to(o))

    def lo_core():
        part = LOA.at[1:8, pl.ds(9 * c, 9)]
        return copy(part, part, lc_s, lc_r, a + 1 - 2 * c, s)

    def lo_core_arrival():
        part = LOA.at[1:8, pl.ds(9 * (1 - c), 9)]
        return copy(part, part, lc_s, lc_r, a + 1 - 2 * c, s)

    loop(1, 16, lambda o: lo_share(o).start())

    def core_share(t):
        return copy(accs.at[t, 1 - c, 0:SENT], crecv.at[t], core_s.at[t], core_r.at[t], a + 1 - 2 * c, s)

    def chip_share(t):
        o = 7 - t
        return copy(isend.at[t], irecv.at[o - 1], ici_s.at[o - 1], ici_r.at[o - 1], chip_to(o) * 2 + c, s)

    def pass_on(t):
        core_share(t).wait_recv()
        isend[t] = accs[t, c, 0:SENT, :] + crecv[t]
        chip_share(t).start()

    def tile(t):
        rows = pl.ds(pl.multiple_of(256 * chip_to(7 - t), 256), 256)
        out = products(AH[rows, :], AL[rows, :])
        accs[t, 0] = out[:, 0:128]
        accs[t, 1] = out[:, 128:256]
        core_share(t).start()

        @pl.when(t > 0)
        def _():
            pass_on(t - 1)

        @pl.when(t == 2)
        def _():
            loop(1, 16, lambda o: lo_share(o).wait_recv())
            lor[0] = lom[a]
            los[...] = jnp.zeros((56, 128), F32)

            def add(k):
                los[...] += lor[(a + 16 - k) % 16]

            loop(0, 16, add)
            LOA[0, a] = los[0:16, :]
            LOA[0, 16] = los[16:32, :]
            LOA[0, 17] = jnp.zeros((16, 128), F32)
            for k in range(3):
                LOA[0, 17, k : k + 1, :] = los[36 + 8 * k : 37 + 8 * k, :]
            loop(1, 16, lambda o: lo_times(o).start())

        @pl.when(t == 4)
        def _():
            loop(1, 16, lambda o: lo_times_arrival(o).wait_recv())
            loop(1, 16, lambda o: lo_times(o).wait_send())
            loop(1, 8, lambda o: lo_space(o).start())

        @pl.when(t == 7)
        def _():
            loop(1, 8, lambda o: lo_space(o).wait_recv())
            lo_core().start()

    loop(0, 8, tile)

    scale = 1.0 / (SLAB * TIMES)
    core_share(7).wait_recv()
    turn[0:SENT, :] = accs[7, c, 0:SENT, :] + crecv[7]

    def add_chip(o):
        chip_share(7 - o).wait_recv()
        turn[0:SENT, :] += irecv[o - 1]

    loop(1, 8, add_chip)
    left, right, four = (turn[128 * k : 128 * k + 128, :].T for k in range(3))

    def place(left, right, four):
        low = lax.broadcasted_iota(jnp.int32, left.shape, 1) < 2
        moved = pltpu.roll(right, 2, 1)
        return left * scale, jnp.where(low, four, moved) * scale, jnp.where(low, moved, four) * scale

    first, second, third = place(left, right, four)
    gram_o[0:128, 0:128] = first
    gram_o[0:128, 128:256] = second
    gram_o[0:128, 256:260] = third[:, 0:4]
    parts = place(los[32:40, :], los[40:48, :], los[48:56, :])
    first, second, third = (jnp.where(c == 0, part[0:2, :], part[2:4, :]) for part in parts)
    gram_o[128:130, 0:128] = first
    gram_o[128:130, 128:256] = second
    gram_o[128:130, 256:260] = third[:, 0:4]

    lo_core_arrival().wait_recv()

    def give(o):
        lo_o[space_from(o)] = LOA[o] * scale

    loop(0, 8, give)

    loop(0, 7, lambda k: share(k).wait_send())
    loop(1, 8, lambda o: spread(o).wait_send())
    loop(1, 16, lambda o: lo_share(o).wait_send())
    loop(1, 8, lambda o: lo_space(o).wait_send())
    lo_core().wait_send()
    loop(0, 8, lambda t: core_share(t).wait_send())
    loop(0, 7, lambda t: chip_share(t).wait_send())


def body(snapshots, basis):
    vmem = pl.BlockSpec(memory_space=pltpu.VMEM)
    dma = pltpu.SemaphoreType.DMA
    rates, gram_quad, lo = pl.pallas_call(
        kernel,
        out_shape=(
            jax.ShapeDtypeStruct((MODES, BLOCK), F32),
            jax.ShapeDtypeStruct((130, 260), F32),
            jax.ShapeDtypeStruct((8, 18, 16, 128), F32),
        ),
        in_specs=[pl.BlockSpec(memory_space=pl.ANY), vmem],
        out_specs=(vmem, vmem, vmem),
        scratch_shapes=[
            pltpu.VMEM((2048, SLAB), BF16),
            pltpu.VMEM((2048, SLAB), BF16),
            pltpu.VMEM((MINE, SLAB), BF16),
            pltpu.VMEM((MINE, SLAB), BF16),
            pltpu.VMEM((256, SLAB), BF16),
            pltpu.VMEM((256, SLAB), BF16),
            pltpu.VMEM((MODES, 2048), BF16),
            pltpu.VMEM((10, MODES, BLOCK), F32),
            pltpu.VMEM((8, 80, BLOCK), F32),
            pltpu.VMEM((64, BLOCK), F32),
            pltpu.VMEM((8, MODES, BLOCK), F32),
            pltpu.VMEM((7, MODES, BLOCK), F32),
            pltpu.VMEM((8, 2, MINE, 128), F32),
            pltpu.VMEM((8, SENT, 128), F32),
            pltpu.VMEM((7, SENT, 128), F32),
            pltpu.VMEM((7, SENT, 128), F32),
            pltpu.VMEM((MINE, 256), F32),
            pltpu.VMEM((384, 128), F32),
            pltpu.VMEM((16, 56, 128), F32),
            pltpu.VMEM((16, 56, 128), F32),
            pltpu.VMEM((56, 128), F32),
            pltpu.VMEM((8, 18, 16, 128), F32),
            dma((8,)), dma((7,)), dma((7,)), dma((7,)), dma((7,)), dma((2,)), dma((2,)),
            dma((8,)), dma((8,)), dma((7,)), dma((7,)),
            dma((15,)), dma((15,)), dma((15,)), dma((15,)), dma((7,)), dma((7,)), dma(()), dma(()),
        ],
        compiler_params=pltpu.CompilerParams(
            collective_id=0, has_side_effects=True, vmem_limit_bytes=60 << 20
        ),
    )(snapshots, basis)
    rows = lo[:, :16].reshape(8, 256, 128)
    extra = lo[:, 16]
    ones = lo[:, 17]
    quad = jnp.concatenate([rows[:, :128], extra[:, 0:2], rows[:, 128:], extra[:, 2:4]], axis=1)
    feats = jnp.concatenate([quad.reshape(2080, 128), extra[0, 4:5], extra[:, 8:16].reshape(64, 128)], axis=0)
    rhs = feats[:, 64:128]
    ones_quad = jnp.concatenate([ones[:, 0], ones[:, 2, 0:2], ones[:, 1], ones[:, 2, 2:4]], axis=1).reshape(1, 2080)
    ones_row = jnp.concatenate([ones_quad, jnp.ones((1, 1), F32), extra[0, 4:5, 0:64]], axis=1)
    side = jnp.concatenate([ones_row, feats[:, 0:64].T], axis=0)
    return rates, gram_quad, side, rhs


def solution(mesh):
    in_specs = (P("space", "tm"), P("space", None))
    out_specs = (P(None, ("tm", "space")), P("tm", "space"), P(), P())
    return jax.shard_map(body, mesh=mesh, in_specs=in_specs, out_specs=out_specs, check_vma=False)
```

time: 660 us -> 97.5 us (0.15)
  waiting for transfers between devices: 299 us -> 0 us
  blocking collectives: 207 us -> 0 us
  Pallas kernels: 0 us -> 84.2 us
  matrix products: 55.9 us -> 0 us
  local copies, waits for them, and re-layouts: 48.2 us -> 11.7 us
  starting transfers between devices: 19.2 us -> 0 us
  between operations: 15.3 us -> 0.74 us
  other arithmetic: 10.4 us -> 0.51 us
    psum x2 -> x0, waiting for transfers between devices: 214 us -> none  [the longest x1 128 us: body(): side_total, rhs_total = lax.psum((side_part, rhs_part), ('tm', 'space'))]
    unnamed x1 -> x0, blocking collectives: 207 us -> none
    pallas_call x0 -> x1, Pallas kernels: none -> 84.2 us  [body(): pl.pallas_call(kernel, out_shape=(jax.ShapeDtypeStruct((MODES, BLOCK), F3...]
    unnamed x6 -> x0, waiting for transfers between devices: 81.2 us -> none
    dot_general x4 -> x0, matrix products: 55.9 us -> none  [the longest x1 34.2 us: body(): quad_part = lax.dot_general(quad, quad, dims, precision=high)]
    gather x2 -> x0, local copies, waits for them, and re-layouts: 13.6 us -> none  [body(): quad = reduced[upper_i] * reduced[upper_j]]
    concatenate x2 -> x3, local copies, waits for them, and re-layouts: 14.2 us -> 0.94 us  [the longest x2 0.49 us: body(): jnp.concatenate([ones_quad, jnp.ones((1, 1), F32), extra[0, 4:5, 0:64]],...]
    unnamed x23 -> x9, local copies, waits for them, and re-layouts: 19.4 us -> 6.91 us
  transfers between devices with their start and end apart: 7 -> 0, of which waited for: 4 -> 0; matrix products, arithmetic and copies ran while one was open for 7% -> 0% of each run, Pallas kernels for 0% -> 0%
where the time goes in v1:
time: 97.5 us; the launch traced here: 97.2 us
  Pallas kernels  84.2 us (86%)
  local copies, waits for them, and re-layouts  11.7 us (12%)
    pallas_call x1, Pallas kernels, body(): pl.pallas_call(kernel, out_shape=(jax.ShapeDtypeStruct((MODES, BLOCK), F3...  84.2 us
    unnamed x9, local copies, waits for them, and re-layouts  6.91 us

profile of v1, /device:TPU:1, one launch (start us, length us, event | category | flops | bytes accessed | tf_op | source)
XLA Modules:
  0.0 97.2 jit_solution(2078399070522696411)
XLA Ops:
  0.6 2.0 %copy.25.basis = bf16[2048,64]{1,0:T(8,128)(2,1)} copy(bf16[2048,64]{0,1:T(8,128)(2,1)} %param.3) | data formatting | bytes 524288 | tf_op args[1]
  2.6 84.2 %shard_map.57 = (f32[64,512]{1,0:T(8,128)}, f32[130,260]{1,0:T(8,128)}, f32[8,18,16,128]{3,2,1,0:T(8,128)}) custom-call(bf16[2048,4096]{1,0:T(8,128)(2,1)} %snap.1, bf16[2048,64]{1,0:T(8,128)(2,1)} %copy.25.basis), custom_call_target="tpu_custom_call" | custom-call | tf_op jit(solution)/shard_map/pallas_call | solution.py:385
  86.8 0.9 slice_bitcast_fusion.2
  87.7 1.3 %slice.55 = f32[8,16,16,128]{3,2,1,0:T(8,128)S(1)} slice(f32[8,18,16,128]{3,2,1,0:T(8,128)} %get-tuple-element.9), slice={[0:8], [0:16], [0:16], [0:128]} | slice | bytes 2097152 | tf_op jit(solution)/shard_map/slice | solution.py:425
  89.0 0.1 fusion.1
  89.1 0.1 fusion.3
  89.2 0.1 pad_maximum_fusion.2
  89.3 0.1 reshape.20
  89.4 0.1 concatenate.16
  89.5 0.1 pad_maximum_fusion.1
  89.6 0.1 reshape.22
  89.6 0.5 concatenate.18
  90.1 0.4 copy.31
  90.5 1.4 %fusion = (f32[2145,64]{1,0:T(8,128)}, f32[64,2145]{0,1:T(8,128)S(1)}) fusion(f32[2145,128]{1,0:T(8,128)S(1)} %concatenate.18), kind=kLoop, calls=%fused_computation.9 | loop fusion | bytes 2196480 | tf_op jit(solution)/shard_map/slice | solution.py:430
  91.9 2.4 %copy.33 = f32[2145,64]{0,1:T(8,128)} copy(f32[2145,64]{1,0:T(8,128)} %get-tuple-element.20) | data formatting | bytes 1098240
  94.3 0.4 pad_maximum_fusion
  94.6 0.0 copy-start.1
  94.6 0.0 copy-start
  94.6 1.2 %copy.32 = f32[65,2145]{1,0:T(8,128)} copy(f32[65,2145]{0,1:T(8,128)S(1)} %pad_maximum_fusion) | data formatting | bytes 1115400
  95.8 0.0 copy-done.1
  95.8 0.7 copy.39
  96.5 0.0 copy-done
  96.5 0.7 copy.40
  (5 shorter events, 0.0 us)
Async XLA Ops:
  94.6 1.2 %copy-start.1 = (f32[64,512]{1,0:T(8,128)S(1)}, f32[64,512]{1,0:T(8,128)}, u32[]{:S(2)}) copy-start(f32[64,512]{1,0:T(8,128)} %get-tuple-element.34) | copy-start | bytes 393220
  94.6 1.9 %copy-start = (f32[130,260]{1,0:T(8,128)S(1)}, f32[130,260]{1,0:T(8,128)}, u32[]{:S(2)}) copy-start(f32[130,260]{1,0:T(8,128)} %get-tuple-element.35) | copy-start | bytes 405604

commit v2 on v1

v2 whole, which is shorter than its diff:
```python
import functools

import jax
import jax.numpy as jnp
import numpy as np
from jax import lax
from jax.experimental import pallas as pl
from jax.experimental.pallas import tpu as pltpu
from jax.sharding import PartitionSpec as P

F32 = jnp.float32
BF16 = jnp.bfloat16
MESH = pl.DeviceIdType.MESH
ROWS_BY_ROWS = (((1,), (1,)), ((), ()))

MODES = 64
SPACE = 8
TIMES = 16
BLOCK = 512
HALF = 256
SLAB = SPACE * BLOCK
MINE = 272
SENT = 264


def pair_of(k):
    i = 0
    while k >= MODES - i:
        k -= MODES - i
        i += 1
    return i, i + k


def half_plan(row):
    block, inside = divmod(row, 128)
    runs = []
    for r in range(8):
        i, j = pair_of(130 * block + inside + r)
        if not runs or runs[-1][1] != i:
            at = j - r + 8
            runs.append((r, i, at % 8, at - at % 8))
    return runs


def build_plan():
    segments = []
    for row in range(0, 2048, 16):
        low, high = half_plan(row), half_plan(row + 8)
        pure = len(low) == 1 and len(high) == 1 and low[0][1:3] == high[0][1:3]
        if not pure:
            segments.append((row, 16, (low, high)))
            continue
        run = low[0]
        last = segments[-1] if segments else None
        if (
            last
            and not isinstance(last[2], tuple)
            and last[2][0] == list(run)[1]
            and last[2][1] == run[2]
            and last[2][2] + last[1] == run[3]
        ):
            segments[-1] = (last[0], last[1] + 16, last[2])
        else:
            segments.append((row, 16, [run[1], run[2], run[3]]))
    return segments


def kernel(
    snap, basis, rates_o, gram_o, side_o, rhs_o,
    AH, AL, MH, ML, LH, LL, XA, XS, LQ, sbuf, rbuf, accs, crecv, yrecv, xsend, xrecv,
    accl, turn, lom, lomr, lor, los, LOT, LOA, GS,
    snap_sem, rs_s, rs_r, ag_s, ag_r, halo_s, halo_r, core_s, core_r, y_s, y_r, x_s, x_r,
    lo_s, lo_r, lt_s, lt_r, lx_s, lx_r, lc_s, lc_r,
):
    a = lax.axis_index("tm")
    s = lax.axis_index("space")
    y, xl, c = a // 4, (a // 2) % 2, a % 2
    chip = a // 2
    sibling = a + 1 - 2 * c
    xh, z = s // 4, s % 4

    def space_to(o):
        return ((xh + o // 4) % 2) * 4 + (z + o % 4) % 4

    def space_from(o):
        return ((xh + 2 - o // 4) % 2) * 4 + (z + 4 - o % 4) % 4

    def copy(src, dst, ss, rs, tm, sp):
        return pltpu.make_async_remote_copy(
            src_ref=src, dst_ref=dst, send_sem=ss, recv_sem=rs, device_id=(tm, sp), device_id_type=MESH
        )

    def loop(low, high, step):
        def inner(k, carry):
            step(k)
            return carry

        lax.fori_loop(low, high, inner, 0)

    def half_cols(m):
        return pl.ds(pl.multiple_of(HALF * m, HALF), HALF)

    def fetch(m):
        cols = pl.ds(pl.multiple_of(BLOCK * space_to(7 - m % 8) + HALF * (m // 8), HALF), HALF)
        return pltpu.make_async_copy(snap.at[:, cols], AH.at[:, half_cols(m)], snap_sem.at[m])

    loop(0, 8, lambda m: fetch(m).start())

    barrier = pltpu.get_barrier_semaphore()

    def greet(tm, sp):
        pl.semaphore_signal(barrier, inc=1, device_id=(tm, sp), device_id_type=MESH)

    up, down = (a + 1) % 16, (a + 15) % 16
    loop(1, 8, lambda o: greet(a, space_to(o)))
    loop(1, 8, lambda o: greet(((chip + o) % 8) * 2 + c, s))
    greet(sibling, s)
    greet(up, s)
    greet(down, s)

    loop(8, 16, lambda m: fetch(m).start())

    def project(m):
        fetch(m).wait()
        sbuf[m] = jnp.dot(basis[...], AH[:, half_cols(m)], preferred_element_type=F32)

    def share(q, o):
        at = 8 * q + o
        return copy(sbuf.at[8 * q + 7 - o], rbuf.at[at], rs_s.at[at], rs_r.at[at], a, space_to(o))

    loop(0, 8, project)
    pl.semaphore_wait(barrier, 17)
    loop(0, 7, lambda m: share(0, 7 - m).start())

    def middle(m):
        project(m)

        @pl.when(m < 15)
        def _():
            share(1, 15 - m).start()

    loop(8, 16, middle)

    def spread(q, o):
        mine = XA.at[q, s + 1]
        return copy(mine, mine, ag_s.at[8 * q + o], ag_r.at[8 * q + o], a, space_to(o))

    def arrival(q, o):
        theirs = XA.at[q, space_from(o) + 1]
        return copy(theirs, theirs, ag_s.at[8 * q + o], ag_r.at[8 * q + o], a, space_to(o))

    for q in range(2):
        def add_share(o):
            share(q, o).wait_recv()
            sbuf[8 * q + 7] += rbuf[8 * q + o]

        loop(1, 8, add_share)
        XA[q, s + 1] = sbuf[8 * q + 7]
        loop(1, 8, lambda o: spread(q, o).start())

    segments = build_plan()

    def split(value):
        high = value.astype(BF16)
        return high, (value - high.astype(F32)).astype(BF16)

    LQ[...] = jnp.where(lax.broadcasted_iota(jnp.int32, (64, HALF), 0) % 8 == 4, 1.0, 0.0).astype(F32)
    LH[192:256, :] = jnp.zeros((64, SLAB), BF16)
    LL[192:256, :] = jnp.zeros((64, SLAB), BF16)
    row8 = lax.broadcasted_iota(jnp.int32, (8, HALF), 0)

    def build(q, b):
        cols = half_cols(8 * q + b)
        x = XA[q, b + 1]
        pad = jnp.zeros((8, HALF), F32)
        xp = jnp.concatenate([pad, x, pad], axis=0)
        XS[0] = xp
        for shift in range(1, 8):
            XS[shift] = pltpu.roll(xp, 80 - shift, 0)

        def row(i):
            return XA[q, b + 1, i : i + 1, :]

        def half(runs):
            value = None
            for first, i, shift, base in runs:
                term = row(i) * XS[shift, base : base + 8, :]
                value = term if value is None else jnp.where(row8 >= first, term, value)
            return value

        for first, count, what in segments:
            if isinstance(what, tuple):
                value = jnp.concatenate([half(what[0]), half(what[1])], axis=0)
            else:
                i, shift, base = what
                value = row(i) * XS[shift, base : base + count, :]
            high, low = split(value)
            AH[first : first + count, cols] = high
            AL[first : first + count, cols] = low
        for n in range(8):
            for p, k in enumerate((260 * n + 128, 260 * n + 129, 260 * n + 258, 260 * n + 259)):
                i, j = pair_of(k)
                LQ[8 * n + p : 8 * n + p + 1, :] = row(i) * row(j)
        high, low = split(x)
        LH[0:64, cols] = high
        LL[0:64, cols] = low
        high, low = split(LQ[...])
        LH[128:192, cols] = high
        LL[128:192, cols] = low
        at = pl.multiple_of(8 * s, 8)
        high, low = split(jnp.concatenate([LQ[pl.ds(at, 8), :], XA[q, b + 1, pl.ds(at, 8), :]], axis=0))
        MH[256:272, cols] = high
        ML[256:272, cols] = low

    own = pl.ds(pl.multiple_of(256 * s, 256), 256)

    def build_half(q):
        cols = pl.ds(2048 * q, 2048)
        loop(0, 8, lambda b: build(q, b))
        MH[0:256, cols] = AH[own, cols]
        ML[0:256, cols] = AL[own, cols]

    def products(high, low, cols):
        out = lax.dot_general(MH[:, cols], high, ROWS_BY_ROWS, preferred_element_type=F32)
        out += lax.dot_general(ML[:, cols], high, ROWS_BY_ROWS, preferred_element_type=F32)
        return out + lax.dot_general(MH[:, cols], low, ROWS_BY_ROWS, preferred_element_type=F32)

    def chip_at(o):
        return ((y + o % 4) % 4) * 2 + (xl + o // 4) % 2

    def tile_products(t, cols):
        rows = pl.ds(pl.multiple_of(256 * chip_at(7 - t), 256), 256)
        return products(AH[rows, cols], AL[rows, cols], cols)

    loop(1, 8, lambda o: arrival(0, o).wait_recv())
    build_half(0)

    loop(1, 8, lambda o: arrival(1, o).wait_recv())

    halo = (
        copy(XA.at[1, 8, :, 128:256], XA.at[1, 0, :, 128:256], halo_s.at[0], halo_r.at[0], up, s),
        copy(XA.at[0, 1, :, 0:128], XA.at[0, 9, :, 0:128], halo_s.at[1], halo_r.at[1], down, s),
    )
    halo[0].start()
    halo[1].start()
    build_half(1)
    halo[0].wait()
    halo[1].wait()
    tail = XA[1, 0, :, 128:256]
    ghost = 2.0 * XA[0, 1, :, 0:1] - XA[0, 1, :, 1:2]
    XA[1, 0, :, 128:256] = jnp.where(a == 0, jnp.broadcast_to(ghost, (64, 128)), tail)
    head = XA[0, 9, :, 0:128]
    ghost = 2.0 * XA[1, 8, :, HALF - 1 : HALF] - XA[1, 8, :, HALF - 2 : HALF - 1]
    XA[0, 9, :, 0:128] = jnp.where(a == 15, jnp.broadcast_to(ghost, (64, 128)), head)
    lane = lax.broadcasted_iota(jnp.int32, (64, HALF), 1)

    def rates_of(q, b):
        x = XA[q, b + 1]
        before = XA[1 - q, b + q, :, HALF - 1 : HALF]
        after = XA[1 - q, b + 1 + q, :, 0:1]
        before = jnp.where(lane == 0, jnp.broadcast_to(before, x.shape), pltpu.roll(x, 1, 1))
        after = jnp.where(lane == HALF - 1, jnp.broadcast_to(after, x.shape), pltpu.roll(x, HALF - 1, 1))
        return 0.5 * (after - before)

    for q in range(2):
        def rate_rows(b):
            high, low = split(rates_of(q, b))
            LH[64:128, half_cols(8 * q + b)] = high
            LL[64:128, half_cols(8 * q + b)] = low

        loop(0, 8, rate_rows)
        rates_o[:, HALF * q : HALF * q + HALF] = rates_of(q, s)

    accl[...] = products(LH[...], LL[...], slice(0, SLAB))
    turn[0:272, :] = accl[...]
    turn[272:384, :] = jnp.zeros((112, 256), F32)
    for k in range(3):
        lines = turn[128 * k : 128 * k + 128, 0:128].T
        for t in range(16):
            lom[t % 2, t // 2, k] = lines[8 * t : 8 * t + 8, :]
        lines = turn[128 * k : 128 * k + 128, 128:256].T
        for t in range(8):
            lom[0, t, 3 + k] = lines[8 * t : 8 * t + 8, :]
            lom[1, t, 3 + k] = lines[8 * t : 8 * t + 8, :]

    def lo_pair():
        return copy(lom.at[1 - c], lomr, lc_s.at[8], lc_r.at[8], sibling, s)

    def lo_share(o):
        to = (chip + o) % 8
        return copy(lom.at[c, to], lor.at[o], lo_s.at[o], lo_r.at[o], to * 2 + c, s)

    def lo_times(o):
        part = LOT.at[chip]
        return copy(part, part, lt_s.at[o], lt_r.at[o], ((chip + o) % 8) * 2 + c, s)

    def lo_times_arrival(o):
        part = LOT.at[(chip + 8 - o) % 8]
        return copy(part, part, lt_s.at[o], lt_r.at[o], ((chip + o) % 8) * 2 + c, s)

    def lo_space(o):
        return copy(LOA.at[0, c], LOA.at[o, c], lx_s.at[o], lx_r.at[o], a, space_to(o))

    def lo_core(o):
        return copy(LOA.at[o, c], LOA.at[o, c], lc_s.at[o], lc_r.at[o], sibling, s)

    def lo_core_arrival(o):
        return copy(LOA.at[o, 1 - c], LOA.at[o, 1 - c], lc_s.at[o], lc_r.at[o], sibling, s)

    def lo_step_1():
        lo_pair().wait()
        lom[c] += lomr[...]
        loop(1, 8, lambda o: lo_share(o).start())

    def lo_step_2():
        loop(1, 8, lambda o: lo_share(o).wait_recv())
        lor[0] = lom[c, chip]
        los[...] = jnp.zeros((6, 8, 128), F32)

        def add(k):
            los[...] += lor[(chip + 8 - k) % 8]

        loop(0, 8, add)
        LOT[chip] = los[0:3]
        loop(1, 8, lambda o: lo_times(o).start())

    lane8 = lax.broadcasted_iota(jnp.int32, (8, 128), 1)

    def lo_step_3():
        loop(1, 8, lambda o: lo_times_arrival(o).wait_recv())
        packed = LOT[0, 2]
        for k in range(8):
            LOA[0, c, k] = LOT[k, 0]
            LOA[0, c, 8 + k] = LOT[k, 1]
            if k:
                packed = jnp.where(lane8 // 16 == k, pltpu.roll(LOT[k, 2], 16 * k, 1), packed)
        LOA[0, c, 16] = packed
        LOA[0, c, 17] = jnp.zeros((8, 128), F32)
        for k in range(3):
            LOA[0, c, 17, k : k + 1, :] = los[3 + k, 4:5, :]
        lo_core(0).start()
        loop(1, 8, lambda o: lo_space(o).start())

    def forward(o):
        lo_space(o).wait_recv()
        lo_core(o).start()

    lo_pair().start()

    def core_share(t):
        return copy(accs.at[t, 1 - c, 0:SENT], crecv.at[t], core_s.at[t], core_r.at[t], sibling, s)

    def y_share(o):
        to = ((y + o % 4) % 4) * 4 + xl * 2 + c
        return copy(accs.at[7 - o, c, 0:SENT], yrecv.at[o], y_s.at[o], y_r.at[o], to, s)

    def x_share():
        return copy(xsend, xrecv, x_s, x_r, y * 4 + (1 - xl) * 2 + c, s)

    def pass_on(t):
        core_share(t).wait_recv()
        accs[t, c, 0:SENT, :] += crecv[t]

        @pl.when(t % 4 < 3)
        def _():
            y_share(7 - t).start()

    def add_y(into, low):
        into[0:SENT] = accs[7 - low, c, 0:SENT, :]

        def add(o):
            y_share(o).wait_recv()
            into[0:SENT] += yrecv[o]

        loop(low + 1, low + 4, add)

    def tile(t):
        out = tile_products(t, slice(0, SLAB))
        accs[t, 0] = out[:, 0:128]
        accs[t, 1] = out[:, 128:256]
        core_share(t).start()

        @pl.when(t > 0)
        def _():
            pass_on(t - 1)

        @pl.when(t == 0)
        def _():
            lo_step_1()

        @pl.when(t == 2)
        def _():
            lo_step_2()

        @pl.when(t == 4)
        def _():
            lo_step_3()

        @pl.when(t == 6)
        def _():
            add_y(xsend, 4)
            x_share().start()

        @pl.when(t == 7)
        def _():
            loop(1, 8, forward)

    loop(0, 8, tile)
    pass_on(7)

    scale = 1.0 / (SLAB * TIMES)
    add_y(accl.at[:, 0:128], 0)
    x_share().wait_recv()
    turn[0:SENT, 0:128] = accl[0:SENT, 0:128] + xrecv[...]
    left, right, four = (turn[128 * k : 128 * k + 128, 0:128].T for k in range(3))

    def place(left, right, four):
        low = lax.broadcasted_iota(jnp.int32, left.shape, 1) < 2
        moved = pltpu.roll(right, 2, 1)
        return left, jnp.where(low, four, moved), jnp.where(low, moved, four)

    first, second, third = place(left, right, four)
    gram_o[0:128, 0:128] = first * scale
    gram_o[0:128, 128:256] = second * scale
    gram_o[0:128, 256:260] = third[:, 0:4] * scale
    parts = place(los[3], los[4], los[5])
    first, second, third = (jnp.where(c == 0, part[0:2, :], part[2:4, :]) * scale for part in parts)
    gram_o[128:130, 0:128] = first
    gram_o[128:130, 128:256] = second
    gram_o[128:130, 256:260] = third[:, 0:4]

    loop(0, 8, lambda o: lo_core_arrival(o).wait_recv())

    wide = lax.broadcasted_iota(jnp.int32, (136, 128), 1)
    carried = jnp.zeros((136, 128), F32)
    last = jnp.zeros((136, 128), F32)
    for b in range(8):
        o = ((xh + 2 - b // 4) % 2) * 4 + (z + 4 - b % 4) % 4
        ones = LOA[o, 0, 17]
        left = jnp.concatenate([LOA[o, t % 2, t // 2] for t in range(16)] + [ones], axis=0)
        right = jnp.concatenate([LOA[o, t % 2, 8 + t // 2] for t in range(16)] + [pltpu.roll(ones, 7, 0)], axis=0)
        packed = [LOA[o, t, 16] for t in range(2)]
        four = jnp.concatenate(
            [pltpu.roll(packed[t % 2], (128 - 16 * (t // 2)) % 128, 1) if t // 2 else packed[t % 2] for t in range(16)]
            + [pltpu.roll(ones, 6, 0)],
            axis=0,
        )
        shift = 4 * b
        first, second, third = (pltpu.roll(v, shift, 1) if b else v for v in place(left, right, four))
        GS[:, 256 * b : 256 * b + 128] = jnp.where(wide < shift, carried, first)
        GS[:, 256 * b + 128 : 256 * b + 256] = jnp.where(wide < shift, first, second)
        carried = jnp.where(wide < shift, second, third)
        modes = pltpu.roll(four, 25 + 8 * b, 1)
        last = jnp.where((wide >= 33 + 8 * b) & (wide < 41 + 8 * b), modes, last)
        if b == 7:
            last = jnp.where(wide == 32, pltpu.roll(four, 28, 1), last)
    GS[:, 2048:2176] = jnp.where(wide < 32, carried, last)
    side_o[0:1, :] = GS[128:129, 0:2145] * scale
    side_o[1:65, :] = GS[0:64, 0:2145] * scale
    rhs_o[...] = GS[64:128, 0:2145] * scale

    for q in range(2):
        loop(1, 8, lambda o: share(q, o).wait_send())
        loop(1, 8, lambda o: spread(q, o).wait_send())
    loop(1, 8, lambda o: lo_share(o).wait_send())
    loop(1, 8, lambda o: lo_times(o).wait_send())
    loop(1, 8, lambda o: lo_space(o).wait_send())
    loop(0, 8, lambda o: lo_core(o).wait_send())
    loop(0, 8, lambda t: core_share(t).wait_send())
    loop(1, 4, lambda o: y_share(o).wait_send())
    loop(5, 8, lambda o: y_share(o).wait_send())
    x_share().wait_send()


def body(snapshots, basis):
    vmem = pl.BlockSpec(memory_space=pltpu.VMEM)
    dma = pltpu.SemaphoreType.DMA
    rates, gram_quad, gram_side, rhs = pl.pallas_call(
        kernel,
        out_shape=(
            jax.ShapeDtypeStruct((MODES, BLOCK), F32),
            jax.ShapeDtypeStruct((130, 260), F32),
            jax.ShapeDtypeStruct((65, 2145), F32),
            jax.ShapeDtypeStruct((64, 2145), F32),
        ),
        in_specs=[pl.BlockSpec(memory_space=pl.ANY), vmem],
        out_specs=(vmem, vmem, vmem, vmem),
        scratch_shapes=[
            pltpu.VMEM((2048, SLAB), BF16),
            pltpu.VMEM((2048, SLAB), BF16),
            pltpu.VMEM((MINE, SLAB), BF16),
            pltpu.VMEM((MINE, SLAB), BF16),
            pltpu.VMEM((256, SLAB), BF16),
            pltpu.VMEM((256, SLAB), BF16),
            pltpu.VMEM((2, 10, MODES, HALF), F32),
            pltpu.VMEM((8, 80, HALF), F32),
            pltpu.VMEM((64, HALF), F32),
            pltpu.VMEM((16, MODES, HALF), F32),
            pltpu.VMEM((16, MODES, HALF), F32),
            pltpu.VMEM((8, 2, MINE, 128), F32),
            pltpu.VMEM((8, SENT, 128), F32),
            pltpu.VMEM((8, SENT, 128), F32),
            pltpu.VMEM((SENT, 128), F32),
            pltpu.VMEM((SENT, 128), F32),
            pltpu.VMEM((MINE, 256), F32),
            pltpu.VMEM((384, 256), F32),
            pltpu.VMEM((2, 8, 6, 8, 128), F32),
            pltpu.VMEM((8, 6, 8, 128), F32),
            pltpu.VMEM((8, 6, 8, 128), F32),
            pltpu.VMEM((6, 8, 128), F32),
            pltpu.VMEM((8, 3, 8, 128), F32),
            pltpu.VMEM((8, 2, 18, 8, 128), F32),
            pltpu.VMEM((136, 2176), F32),
            dma((16,)), dma((16,)), dma((16,)), dma((16,)), dma((16,)), dma((2,)), dma((2,)),
            dma((8,)), dma((8,)), dma((8,)), dma((8,)), dma(()), dma(()),
            dma((8,)), dma((8,)), dma((8,)), dma((8,)), dma((8,)), dma((8,)), dma((9,)), dma((9,)),
        ],
        compiler_params=pltpu.CompilerParams(
            collective_id=0, has_side_effects=True, vmem_limit_bytes=60 << 20
        ),
    )(snapshots, basis.T)
    return rates, gram_quad, gram_side, rhs.T


def solution(mesh):
    in_specs = (P("space", "tm"), P("space", None))
    out_specs = (P(None, ("tm", "space")), P("tm", "space"), P(), P())
    return jax.shard_map(body, mesh=mesh, in_specs=in_specs, out_specs=out_specs, check_vma=False)
```

time: 97.5 us -> 81 us (0.83)
  Pallas kernels: 84.2 us -> 73 us
  local copies, waits for them, and re-layouts: 11.7 us -> 7.03 us
    pallas_call x1, Pallas kernels: 84.2 us -> 73 us  [body(): pl.pallas_call(kernel, out_shape=(jax.ShapeDtypeStruct((MODES, BLOCK), F3...]
    slice x6 -> x0, local copies, waits for them, and re-layouts: 2.82 us -> none  [the longest x1 1.36 us: body(): rhs = feats[:, 64:128]]
    unnamed x9 -> x4, local copies, waits for them, and re-layouts: 6.91 us -> 7.03 us
where the time goes in v2:
time: 81 us; the launch traced here: 80.7 us
  Pallas kernels  73 us (90%)
  local copies, waits for them, and re-layouts  7.03 us (9%)
    pallas_call x1, Pallas kernels, body(): pl.pallas_call(kernel, out_shape=(jax.ShapeDtypeStruct((MODES, BLOCK), F3...  73 us
    unnamed x4, local copies, waits for them, and re-layouts  7.03 us

profile of v2, /device:TPU:1, one launch (start us, length us, event | category | flops | bytes accessed | tf_op | source)
XLA Modules:
  0.0 80.7 jit_solution(720980548860180654)
XLA Ops:
  0.6 73.0 %shard_map.57 = (f32[64,512]{1,0:T(8,128)}, f32[130,260]{1,0:T(8,128)}, f32[65,2145]{1,0:T(8,128)}, f32[64,2145]{1,0:T(8,128)}) custom-call(bf16[2048,4096]{1,0:T(8,128)(2,1)} %snap.1, bf16[64,2048]{1,0:T(8,128)(2,1)} %bitcast.3), custom_call_target="tpu_custom_call" | custom-call | tf_op jit(solution)/shard_map/pallas_call | solution.py:478
  73.7 1.6 %copy.10 = f32[64,512]{1,0:T(8,128)} copy(f32[64,512]{1,0:T(8,128)} %get-tuple-element.16) | data formatting | bytes 262144
  75.2 1.6 %copy.11 = f32[130,260]{1,0:T(8,128)} copy(f32[130,260]{1,0:T(8,128)} %get-tuple-element.17) | data formatting | bytes 270400
  76.9 1.9 %copy.12 = f32[65,2145]{1,0:T(8,128)} copy(f32[65,2145]{1,0:T(8,128)} %get-tuple-element.18) | data formatting | bytes 1115400
  78.8 1.9 %copy.13 = f32[2145,64]{0,1:T(8,128)} copy(f32[2145,64]{0,1:T(8,128)} %bitcast.2) | data formatting | bytes 1098240

commit v3 on v2

--- a/solution.py
+++ b/solution.py
@@ -470,6 +470,23 @@
     loop(1, 4, lambda o: y_share(o).wait_send())
     loop(5, 8, lambda o: y_share(o).wait_send())
     x_share().wait_send()
+
+
+def hand_over_kernel(*refs):
+    count = len(refs) // 2
+    for given, final in zip(refs[:count], refs[count:]):
+        final[...] = given[...]
+
+
+def hand_over(*arrays):
+    vmem = pl.BlockSpec(memory_space=pltpu.VMEM)
+    return pl.pallas_call(
+        hand_over_kernel,
+        out_shape=tuple(jax.ShapeDtypeStruct(each.shape, each.dtype) for each in arrays),
+        in_specs=[vmem] * len(arrays),
+        out_specs=(vmem,) * len(arrays),
+        compiler_params=pltpu.CompilerParams(vmem_limit_bytes=16 << 20),
+    )(*arrays)
 
 
 def body(snapshots, basis):
@@ -519,6 +536,7 @@
             collective_id=0, has_side_effects=True, vmem_limit_bytes=60 << 20
         ),
     )(snapshots, basis.T)
+    rates, gram_quad, gram_side, rhs = hand_over(rates, gram_quad, gram_side, rhs)
     return rates, gram_quad, gram_side, rhs.T
 
 

time: 81 us -> 79.1 us (0.977)
  local copies, waits for them, and re-layouts: 7.03 us -> 3.96 us
  Pallas kernels: 73 us -> 74.3 us
    unnamed x4 -> x8, local copies, waits for them, and re-layouts: 7.03 us -> 3.96 us
    pallas_call x0 -> x1, Pallas kernels: none -> 1.22 us  [hand_over(): pl.pallas_call(hand_over_kernel, out_shape=tuple((jax.ShapeDtypeStruct(ea...]
where the time goes in v3:
time: 79.1 us; the launch traced here: 78.9 us
  Pallas kernels  74.3 us (94%)
  local copies, waits for them, and re-layouts  3.96 us (5%)
    pallas_call x1, Pallas kernels, body(): pl.pallas_call(kernel, out_shape=(jax.ShapeDtypeStruct((MODES, BLOCK), F3...  73 us
    unnamed x8, local copies, waits for them, and re-layouts  3.96 us

profile of v3, /device:TPU:1, one launch (start us, length us, event | category | flops | bytes accessed | tf_op | source)
XLA Modules:
  0.0 78.9 jit_solution(13609222494247424848)
XLA Ops:
  0.6 73.0 %shard_map.57 = (f32[64,512]{1,0:T(8,128)}, f32[130,260]{1,0:T(8,128)}, f32[65,2145]{1,0:T(8,128)}, f32[64,2145]{1,0:T(8,128)}) custom-call(bf16[2048,4096]{1,0:T(8,128)(2,1)} %snap.1, bf16[64,2048]{1,0:T(8,128)(2,1)} %bitcast.2), custom_call_target="tpu_custom_call" | custom-call | tf_op jit(solution)/shard_map/pallas_call | solution.py:495
  73.7 0.0 copy-start
  73.7 1.1 %copy-done = f32[65,2145]{1,0:T(8,128)S(1)} copy-done((f32[65,2145]{1,0:T(8,128)S(1)}, f32[65,2145]{1,0:T(8,128)}, u32[]{:S(2)}) %copy-start) | copy-done | bytes 557724
  74.8 0.0 copy-start.1
  74.8 1.1 %copy-done.1 = f32[64,2145]{1,0:T(8,128)S(1)} copy-done((f32[64,2145]{1,0:T(8,128)S(1)}, f32[64,2145]{1,0:T(8,128)}, u32[]{:S(2)}) %copy-start.1) | copy-done | bytes 549144
  75.8 0.0 copy-start.2
  75.8 0.9 %copy-done.2 = f32[130,260]{1,0:T(8,128)S(1)} copy-done((f32[130,260]{1,0:T(8,128)S(1)}, f32[130,260]{1,0:T(8,128)}, u32[]{:S(2)}) %copy-start.2) | copy-done | bytes 135224
  76.7 0.0 copy-start.3
  76.7 0.9 %copy-done.3 = f32[64,512]{1,0:T(8,128)S(1)} copy-done((f32[64,512]{1,0:T(8,128)S(1)}, f32[64,512]{1,0:T(8,128)}, u32[]{:S(2)}) %copy-start.3) | copy-done | bytes 131096
  77.7 1.2 %shard_map.58 = (f32[64,512]{1,0:T(8,128)}, f32[130,260]{1,0:T(8,128)}, f32[65,2145]{1,0:T(8,128)}, f32[64,2145]{1,0:T(8,128)}) custom-call(f32[64,512]{1,0:T(8,128)S(1)} %copy-done.3, f32[130,260]{1,0:T(8,128)S(1)} %copy-done.2, f32[65,2145]{1,0:T(8,128)S(1)} %copy-done, f32[64,2145]{1,0:T(8,128)S(1)} %copy-done.1), custom_call_target="tpu_custom_call" | custom-call | tf_op jit(solution)/shard_map/pallas_call | solution.py:483
Async XLA Ops:
  73.7 1.1 %copy-start = (f32[65,2145]{1,0:T(8,128)S(1)}, f32[65,2145]{1,0:T(8,128)}, u32[]{:S(2)}) copy-start(f32[65,2145]{1,0:T(8,128)} %get-tuple-element.14.refs_2_) | copy-start | bytes 1673104
  74.8 1.1 %copy-start.1 = (f32[64,2145]{1,0:T(8,128)S(1)}, f32[64,2145]{1,0:T(8,128)}, u32[]{:S(2)}) copy-start(f32[64,2145]{1,0:T(8,128)} %get-tuple-element.15.refs_3_) | copy-start | bytes 1647364
  75.8 0.9 %copy-start.2 = (f32[130,260]{1,0:T(8,128)S(1)}, f32[130,260]{1,0:T(8,128)}, u32[]{:S(2)}) copy-start(f32[130,260]{1,0:T(8,128)} %get-tuple-element.13.refs_1_) | copy-start | bytes 405604
  76.7 0.9 %copy-start.3 = (f32[64,512]{1,0:T(8,128)S(1)}, f32[64,512]{1,0:T(8,128)}, u32[]{:S(2)}) copy-start(f32[64,512]{1,0:T(8,128)} %get-tuple-element.12.refs_0_) | copy-start | bytes 393220

commit v4 on v3

--- a/solution.py
+++ b/solution.py
@@ -473,19 +473,30 @@
 
 
 def hand_over_kernel(*refs):
-    count = len(refs) // 2
-    for given, final in zip(refs[:count], refs[count:]):
-        final[...] = given[...]
+    count = (len(refs) - 2) // 3
+    given, final, held = refs[:count], refs[count : 2 * count], refs[2 * count : 3 * count]
+    come, go = refs[-2:]
+    arrive = [pltpu.make_async_copy(given[k], held[k], come.at[k]) for k in range(count)]
+    leave = [pltpu.make_async_copy(held[k], final[k], go.at[k]) for k in range(count)]
+    for each in arrive:
+        each.start()
+    for k in range(count):
+        arrive[k].wait()
+        leave[k].start()
+    for each in leave:
+        each.wait()
 
 
 def hand_over(*arrays):
-    vmem = pl.BlockSpec(memory_space=pltpu.VMEM)
+    anywhere = pl.BlockSpec(memory_space=pl.ANY)
     return pl.pallas_call(
         hand_over_kernel,
         out_shape=tuple(jax.ShapeDtypeStruct(each.shape, each.dtype) for each in arrays),
-        in_specs=[vmem] * len(arrays),
-        out_specs=(vmem,) * len(arrays),
-        compiler_params=pltpu.CompilerParams(vmem_limit_bytes=16 << 20),
+        in_specs=[anywhere] * len(arrays),
+        out_specs=(anywhere,) * len(arrays),
+        scratch_shapes=[pltpu.VMEM(each.shape, each.dtype) for each in arrays]
+        + [pltpu.SemaphoreType.DMA((len(arrays),))] * 2,
+        compiler_params=pltpu.CompilerParams(vmem_limit_bytes=60 << 20),
     )(*arrays)
 
 

time: 79.1 us -> 76.2 us (0.963)
  local copies, waits for them, and re-layouts: 3.96 us -> 0 us
  Pallas kernels: 74.3 us -> 75.4 us
    unnamed x8 -> x0, local copies, waits for them, and re-layouts: 3.96 us -> none
    pallas_call x1, Pallas kernels: 1.22 us -> 2.33 us  [hand_over(): pl.pallas_call(hand_over_kernel, out_shape=tuple((jax.ShapeDtypeStruct(ea...]
where the time goes in v4:
time: 76.2 us; the launch traced here: 76 us
  Pallas kernels  75.4 us (99%)
    pallas_call x1, Pallas kernels, body(): pl.pallas_call(kernel, out_shape=(jax.ShapeDtypeStruct((MODES, BLOCK), F3...  73 us
    pallas_call x1, Pallas kernels, hand_over(): pl.pallas_call(hand_over_kernel, out_shape=tuple((jax.ShapeDtypeStruct(ea...  2.33 us

profile of v4, /device:TPU:1, one launch (start us, length us, event | category | flops | bytes accessed | tf_op | source)
XLA Modules:
  0.0 76.0 jit_solution(12447272867374784830)
XLA Ops:
  0.6 73.0 %shard_map.57 = (f32[64,512]{1,0:T(8,128)}, f32[130,260]{1,0:T(8,128)}, f32[65,2145]{1,0:T(8,128)}, f32[64,2145]{1,0:T(8,128)}) custom-call(bf16[2048,4096]{1,0:T(8,128)(2,1)} %snap.1, bf16[64,2048]{1,0:T(8,128)(2,1)} %bitcast.2), custom_call_target="tpu_custom_call" | custom-call | tf_op jit(solution)/shard_map/pallas_call | solution.py:506
  73.7 2.3 %shard_map.58 = (f32[64,512]{1,0:T(8,128)}, f32[130,260]{1,0:T(8,128)}, f32[65,2145]{1,0:T(8,128)}, f32[64,2145]{1,0:T(8,128)}) custom-call(f32[64,512]{1,0:T(8,128)} %get-tuple-element.12.refs_0_, f32[130,260]{1,0:T(8,128)} %get-tuple-element.13.refs_1_, f32[65,2145]{1,0:T(8,128)} %get-tuple-element.14.refs_2_, f32[64,2145]{1,0:T(8,128)} %get-tuple-element.15.refs_3_), custom_call_target="tpu_custom_call" | custom-call | tf_op jit(solution)/shard_map/pallas_call | solution.py:492

commit v5 on v4

--- a/solution.py
+++ b/solution.py
@@ -114,7 +114,6 @@
     up, down = (a + 1) % 16, (a + 15) % 16
     loop(1, 8, lambda o: greet(a, space_to(o)))
     loop(1, 8, lambda o: greet(((chip + o) % 8) * 2 + c, s))
-    greet(sibling, s)
     greet(up, s)
     greet(down, s)
 
@@ -129,7 +128,7 @@
         return copy(sbuf.at[8 * q + 7 - o], rbuf.at[at], rs_s.at[at], rs_r.at[at], a, space_to(o))
 
     loop(0, 8, project)
-    pl.semaphore_wait(barrier, 17)
+    pl.semaphore_wait(barrier, 16)
     loop(0, 7, lambda m: share(0, 7 - m).start())
 
     def middle(m):
@@ -375,12 +374,16 @@
         loop(low + 1, low + 4, add)
 
     def tile(t):
+        @pl.when(t == 7)
+        def _():
+            pass_on(6)
+
         out = tile_products(t, slice(0, SLAB))
         accs[t, 0] = out[:, 0:128]
         accs[t, 1] = out[:, 128:256]
         core_share(t).start()
 
-        @pl.when(t > 0)
+        @pl.when((t > 0) & (t < 7))
         def _():
             pass_on(t - 1)
 

time: 76.2 us -> 76.7 us (level)
  no operation moved by 1% of the time
where the time goes in v5:
time: 76.7 us; the launch traced here: 76.5 us
  Pallas kernels  75.8 us (99%)
    pallas_call x1, Pallas kernels, body(): pl.pallas_call(kernel, out_shape=(jax.ShapeDtypeStruct((MODES, BLOCK), F3...  73.5 us
    pallas_call x1, Pallas kernels, hand_over(): pl.pallas_call(hand_over_kernel, out_shape=tuple((jax.ShapeDtypeStruct(ea...  2.33 us

profile of v5, /device:TPU:1, one launch (start us, length us, event | category | flops | bytes accessed | tf_op | source)
XLA Modules:
  0.0 76.5 jit_solution(3640079767940997531)
XLA Ops:
  0.6 73.5 %shard_map.57 = (f32[64,512]{1,0:T(8,128)}, f32[130,260]{1,0:T(8,128)}, f32[65,2145]{1,0:T(8,128)}, f32[64,2145]{1,0:T(8,128)}) custom-call(bf16[2048,4096]{1,0:T(8,128)(2,1)} %snap.1, bf16[64,2048]{1,0:T(8,128)(2,1)} %bitcast.2), custom_call_target="tpu_custom_call" | custom-call | tf_op jit(solution)/shard_map/pallas_call | solution.py:509
  74.2 2.3 %shard_map.58 = (f32[64,512]{1,0:T(8,128)}, f32[130,260]{1,0:T(8,128)}, f32[65,2145]{1,0:T(8,128)}, f32[64,2145]{1,0:T(8,128)}) custom-call(f32[64,512]{1,0:T(8,128)} %get-tuple-element.12.refs_0_, f32[130,260]{1,0:T(8,128)} %get-tuple-element.13.refs_1_, f32[65,2145]{1,0:T(8,128)} %get-tuple-element.14.refs_2_, f32[64,2145]{1,0:T(8,128)} %get-tuple-element.15.refs_3_), custom_call_target="tpu_custom_call" | custom-call | tf_op jit(solution)/shard_map/pallas_call | solution.py:495
